TPU v7x, 1024 devices: a whole 4x4x32 slice. The times are simulated.
1024 devices in a mesh: blk: 128 (over z_lo, x, core), grp: 8 (over z_hi, y).
Axes of the slice: x: 4, y: 4, z: 32 (z_hi: 2, z_lo: 16; z = z_hi * 16 + z_lo), core: 2. Of those that a mesh axis runs over, the one named last changes fastest.
Arguments:
- image_emb: bfloat16 [131072, 1152], P(('blk', 'grp')), may hold values from -0.19921875 to 0.19921875
- text_emb: bfloat16 [131072, 1152], P(('blk', 'grp')), may hold values from -0.19921875 to 0.19921875
- loop_mask: int32 [1024, 4], P(('blk', 'grp')), may hold values from 0 to 1, as said below
- neg_list: int32 [1024, 2], P(('blk', 'grp')), may hold values from 0 to 7, as said below
Outputs:
- row_loss: float32 [131072], P(('blk', 'grp'))
- image_grad: bfloat16 [131072, 1152], P(('blk', 'grp'))
- text_grad: bfloat16 [131072, 1152], P(('blk', 'grp'))
Inputs may be any that keep to these rules, and one draw needn't show every extreme that they name: `loop_mask`: 1 marks a scored pair of blocks, 0 an unscored one. `neg_list`: the 2 entries of a row are distinct and differ from the row's own group index, k mod 8.
All inputs are finite; a program needn't handle non-finite values.
Results may differ from a plain program's by a relative error of at most 0.013.
Values may be sent and summed in bfloat16 or wider, within the bound.
A program may use at most 32 MiB of HBM per device.

v0:
```python
import jax
import jax.numpy as jnp
from jax import lax
from jax.sharding import PartitionSpec as P

HALF = 2


epsilon = 1e-06
logit_scale = 16.0
logit_bias = -2.0


def passed_along(block, axis, distance):
    devices = range(lax.axis_size(axis))
    route = [((i - distance) % len(devices), i) for i in devices]
    return lax.ppermute(block, axis, route)


def normalize(embedding):
    values = embedding.astype(jnp.float32)
    magnitude = jnp.sqrt(jnp.sum(values * values, axis=-1, keepdims=True) + epsilon)
    unit_full = values / magnitude
    return (magnitude, unit_full, unit_full.astype(jnp.bfloat16))


def unit_backward(unit_full, magnitude, unit_grad):
    along = jnp.sum(unit_full * unit_grad, axis=-1, keepdims=True)
    return ((unit_grad - unit_full * along) / magnitude).astype(jnp.bfloat16)


def pair_terms(image_unit, text_block, col_weight, own_block):
    scores = (
        logit_scale
        * lax.dot_general(
            image_unit, text_block, (((1,), (1,)), ((), ())), preferred_element_type=jnp.float32
        )
        + logit_bias
    )
    pair_grad = jax.nn.sigmoid(scores)
    losses = jnp.sum(jax.nn.softplus(scores) * col_weight[None, :], axis=1)
    if own_block:
        pair_grad = pair_grad - jnp.eye(scores.shape[0], dtype=jnp.float32)
        losses = losses - jnp.diagonal(scores)
    grad_half = (pair_grad * col_weight[None, :]).astype(jnp.bfloat16)
    image_part = logit_scale * jnp.dot(grad_half, text_block, preferred_element_type=jnp.float32)
    text_part = logit_scale * lax.dot_general(
        grad_half, image_unit, (((0,), (0,)), ((), ())), preferred_element_type=jnp.float32
    )
    return (losses, image_part, text_part)


def scored_pair(image_unit, visitor, loop_mask, offset):
    mask_col = offset + HALF if offset < 0 else offset + HALF - 1
    weight = loop_mask[0, mask_col].astype(jnp.float32)
    col_weight = jnp.full((visitor.shape[0],), weight, jnp.float32)
    return pair_terms(image_unit, visitor, col_weight, False)


def move_text(block, hop):
    return passed_along(block, "blk", hop)


def move_grad(block, hop):
    return passed_along(block.astype(jnp.bfloat16), "blk", hop).astype(block.dtype)


def move_home(block, hop):
    return passed_along(block.astype(jnp.bfloat16), "blk", hop).astype(block.dtype)


def on_device(image_emb, text_emb, loop_mask, neg_list):
    row_count = image_emb.shape[0]
    image_mag, image_full, image_unit = normalize(image_emb)
    text_mag, text_full, text_unit = normalize(text_emb)
    all_ones = jnp.ones((row_count,), jnp.float32)
    losses, image_sum, text_sum = pair_terms(image_unit, text_unit, all_ones, True)
    offsets = list(range(-HALF, 0)) + list(range(1, HALF + 1))
    visitor = move_text(text_unit, HALF)
    carried = jnp.zeros(text_unit.shape, jnp.float32)
    for position, offset in enumerate(offsets):
        if position > 0:
            hop = -2 if offsets[position - 1] == -1 else -1
            visitor = move_text(visitor, hop)
            carried = move_grad(carried, hop)
        part_loss, image_part, text_part = scored_pair(image_unit, visitor, loop_mask, offset)
        losses = losses + part_loss
        image_sum = image_sum + image_part
        carried = carried + text_part
    text_sum = text_sum + move_home(carried, HALF)
    hard_picks = neg_list[0]
    shard_rows = lax.all_gather(text_unit, "grp", axis=0, tiled=True)
    loss_sum = losses
    image_acc = image_sum
    block_ids = jnp.arange(shard_rows.shape[0], dtype=jnp.int32) // row_count
    col_weight = jnp.any(block_ids[:, None] == hard_picks[None, :], axis=1).astype(jnp.float32)
    part_loss, image_part, text_part = pair_terms(image_unit, shard_rows, col_weight, False)
    group_grads = text_part.astype(jnp.bfloat16)
    losses, image_sum, group_grads = (loss_sum + part_loss, image_acc + image_part, group_grads)
    text_sum = text_sum + lax.psum_scatter(
        group_grads.astype(jnp.float32).astype(jnp.bfloat16), "grp", scatter_dimension=0, tiled=True
    ).astype(jnp.float32)
    image_grad = unit_backward(image_full, image_mag, image_sum)
    text_grad = unit_backward(text_full, text_mag, text_sum)
    return (losses, image_grad, text_grad)


def solution(mesh):
    placed = (
        P(("blk", "grp"), None),
        P(("blk", "grp"), None),
        P(("blk", "grp"), None),
        P(("blk", "grp"), None),
    )
    return jax.shard_map(
        on_device,
        mesh=mesh,
        in_specs=placed,
        out_specs=(P(("blk", "grp")), P(("blk", "grp"), None), P(("blk", "grp"), None)),
        check_vma=False,
    )
```

profile of v0, /device:TPU:1, one launch (start us, length us, event | category | flops | bytes accessed | tf_op | source)
XLA Modules:
  0.0 530.4 jit_solution(8739383678032061651)
XLA Ops:
  7.2 1.1 fusion.11
  8.3 1.8 fusion.28
  10.2 4.1 collective-permute-start
  14.3 1.4 fusion.30
  15.7 0.7 compare_reduce_fusion
  16.5 1.1 fusion.10
  17.6 1.1 fusion.27
  18.7 1.3 fusion.14
  22.4 1.3 gather_fusion
  24.0 19.8 %collective-permute-done = bf16[128,1152]{1,0:T(8,128)(2,1)S(1)} collective-permute-done((bf16[128,1152]{1,0:T(8,128)(2,1)}, bf16[128,1152]{1,0:T(8,128)(2,1)S(1)}, u32[]{:S(2)}, u32[]{:S(2)}) %collective-permute-start) | collective-permute-done | bytes 294944 | tf_op jit(solution)/shard_map/ppermute | solution.py:17
  43.8 9.7 %collective-permute-start.1 = (bf16[128,1152]{1,0:T(8,128)(2,1)S(1)}, bf16[128,1152]{1,0:T(8,128)(2,1)S(1)}, u32[]{:S(2)}, u32[]{:S(2)}) collective-permute-start(bf16[128,1152]{1,0:T(8,128)(2,1)S(1)} %collective-permute-done), channel_id=1, source_target_pairs={{8,0},{16,8},{24,16},{32,24},{40,32},{48,40},{56,48},{64,56},{72,6... | collective-permute-start | bytes 884744 | tf_op jit(solution)/shard_map/ppermute | solution.py:17
  53.9 187.1 %all-gather.2.cloned.1.call-done = bf16[1024,1152]{1,0:T(8,128)(2,1)} async-done(((bf16[128,1152]{1,0:T(8,128)(2,1)}), bf16[1024,1152]{1,0:T(8,128)(2,1)}) %all-gather.2.cloned.1.call-update) | async-done | bytes 2359312 | tf_op jit(solution)/shard_map/all_gather | solution.py:92
  241.0 2.8 fusion.13
  243.8 2.2 fusion
  246.3 3.3 collective-permute-start.4
  249.9 5.2 collective-permute-start.2
  255.4 0.5 collective-permute-done.4
  256.1 21.9 %collective-permute-start.5 = (bf16[128,1152]{1,0:T(8,128)(2,1)S(1)}, bf16[128,1152]{1,0:T(8,128)(2,1)S(1)}, u32[]{:S(2)}, u32[]{:S(2)}) collective-permute-start(bf16[128,1152]{1,0:T(8,128)(2,1)S(1)} %add_convert_fusion.2), channel_id=1, source_target_pairs={{16,0},{24,8},{32,16},{40,24},{48,32},{56,40},{64,48},{72,56},{80,... | collective-permute-start | bytes 884744 | tf_op jit(solution)/shard_map/ppermute | solution.py:17
  278.3 1.9 collective-permute-start.3
  280.7 3.6 collective-permute-done.5
  284.4 3.9 collective-permute-start.6
  288.6 0.3 fusion.22
  289.1 3.8 collective-permute-done.6
  293.0 2.1 collective-permute-start.7
  295.1 0.6 fusion.29
  295.7 0.4 multiply_reduce_fusion.1
  296.1 0.9 divide_convert_fusion.1
  297.0 0.5 add_add_fusion
  297.5 60.1 %collective-permute-done.7 = bf16[128,1152]{1,0:T(8,128)(2,1)S(1)} collective-permute-done((bf16[128,1152]{1,0:T(8,128)(2,1)S(1)}, bf16[128,1152]{1,0:T(8,128)(2,1)S(1)}, u32[]{:S(2)}, u32[]{:S(2)}) %collective-permute-start.7) | collective-permute-done | bytes 294944 | tf_op jit(solution)/shard_map/ppermute | solution.py:17
  357.7 163.5 %reduce-scatter.2.cloned.1.call-done = bf16[128,1152]{1,0:T(8,128)(2,1)} async-done(((bf16[1024,1152]{1,0:T(8,128)(2,1)}), bf16[128,1152]{1,0:T(8,128)(2,1)}) %reduce-scatter.2.cloned.1.call-update) | async-done | bytes 294928 | tf_op jit(solution)/shard_map/reduce_scatter | solution.py:100
  521.1 1.4 multiply_reduce_fusion
  522.6 0.9 divide_convert_fusion
  (35 shorter events, 3.2 us)
Async XLA Ops:
  7.2 233.8 %all-gather.2.cloned.1.call-start = ((), (), s32[]{:S(2)}) async-start(), calls=%async_computation.1 | async-start | bytes 2654208 | tf_op jit(solution)/shard_map/all_gather | solution.py:92
  10.1 13.6 %copy-start.2 = (bf16[128,1152]{1,0:T(8,128)(2,1)S(1)}, bf16[128,1152]{1,0:T(8,128)(2,1)}, u32[]{:S(2)}) copy-start(bf16[128,1152]{1,0:T(8,128)(2,1)} %fusion.28) | copy-start | bytes 884740
  10.2 511.0 %reduce-scatter.2.cloned.1.call-start = ((), (), s32[]{:S(2)}) async-start(), calls=%async_computation.2 | async-start | bytes 2654208 | tf_op jit(solution)/shard_map/reduce_scatter | solution.py:100
  10.2 33.6 %collective-permute-start = (bf16[128,1152]{1,0:T(8,128)(2,1)}, bf16[128,1152]{1,0:T(8,128)(2,1)S(1)}, u32[]{:S(2)}, u32[]{:S(2)}) collective-permute-start(bf16[128,1152]{1,0:T(8,128)(2,1)} %fusion.28), channel_id=1, source_target_pairs={{1008,0},{1016,8},{0,16},{8,24},{16,32},{24,40},{32,48},{40,56},{4... | collective-permute-start | bytes 884744 | tf_op jit(solution)/shard_map/ppermute | solution.py:17
  43.8 206.1 %collective-permute-start.1 = (bf16[128,1152]{1,0:T(8,128)(2,1)S(1)}, bf16[128,1152]{1,0:T(8,128)(2,1)S(1)}, u32[]{:S(2)}, u32[]{:S(2)}) collective-permute-start(bf16[128,1152]{1,0:T(8,128)(2,1)S(1)} %collective-permute-done), channel_id=1, source_target_pairs={{8,0},{16,8},{24,16},{32,24},{40,32},{48,40},{56,48},{64,56},{72,6... | collective-permute-start | bytes 884744 | tf_op jit(solution)/shard_map/ppermute | solution.py:17
  246.3 9.5 %collective-permute-start.4 = (bf16[128,1152]{1,0:T(8,128)(2,1)S(1)}, bf16[128,1152]{1,0:T(8,128)(2,1)S(1)}, u32[]{:S(2)}, u32[]{:S(2)}) collective-permute-start(bf16[128,1152]{1,0:T(8,128)(2,1)S(1)} %fusion.3), channel_id=1, source_target_pairs={{8,0},{16,8},{24,16},{32,24},{40,32},{48,40},{56,48},{64,56},{72,6... | collective-permute-start | bytes 884744 | tf_op jit(solution)/shard_map/ppermute | solution.py:17
  249.9 28.4 %collective-permute-start.2 = (bf16[128,1152]{1,0:T(8,128)(2,1)S(1)}, bf16[128,1152]{1,0:T(8,128)(2,1)S(1)}, u32[]{:S(2)}, u32[]{:S(2)}) collective-permute-start(bf16[128,1152]{1,0:T(8,128)(2,1)S(1)} %collective-permute-done.1), channel_id=1, source_target_pairs={{16,0},{24,8},{32,16},{40,24},{48,32},{56,40},{64,48},{72,56},{80,... | collective-permute-start | bytes 884744 | tf_op jit(solution)/shard_map/ppermute | solution.py:17
  256.1 28.2 %collective-permute-start.5 = (bf16[128,1152]{1,0:T(8,128)(2,1)S(1)}, bf16[128,1152]{1,0:T(8,128)(2,1)S(1)}, u32[]{:S(2)}, u32[]{:S(2)}) collective-permute-start(bf16[128,1152]{1,0:T(8,128)(2,1)S(1)} %add_convert_fusion.2), channel_id=1, source_target_pairs={{16,0},{24,8},{32,16},{40,24},{48,32},{56,40},{64,48},{72,56},{80,... | collective-permute-start | bytes 884744 | tf_op jit(solution)/shard_map/ppermute | solution.py:17
  278.3 10.3 %collective-permute-start.3 = (bf16[128,1152]{1,0:T(8,128)(2,1)S(1)}, bf16[128,1152]{1,0:T(8,128)(2,1)S(1)}, u32[]{:S(2)}, u32[]{:S(2)}) collective-permute-start(bf16[128,1152]{1,0:T(8,128)(2,1)S(1)} %collective-permute-done.2), channel_id=1, source_target_pairs={{8,0},{16,8},{24,16},{32,24},{40,32},{48,40},{56,48},{64,56},{72,6... | collective-permute-start | bytes 884744 | tf_op jit(solution)/shard_map/ppermute | solution.py:17
  284.4 10.7 %copy-start.4 = (bf16[1024,1152]{1,0:T(8,128)(2,1)S(1)}, bf16[1024,1152]{1,0:T(8,128)(2,1)}, u32[]{:S(2)}) copy-start(bf16[1024,1152]{1,0:T(8,128)(2,1)} %all-gather.2.cloned.1.call-done) | copy-start | bytes 7077892
  284.4 8.6 %collective-permute-start.6 = (bf16[128,1152]{1,0:T(8,128)(2,1)S(1)}, bf16[128,1152]{1,0:T(8,128)(2,1)S(1)}, u32[]{:S(2)}, u32[]{:S(2)}) collective-permute-start(bf16[128,1152]{1,0:T(8,128)(2,1)S(1)} %add_convert_fusion.1), channel_id=1, source_target_pairs={{8,0},{16,8},{24,16},{32,24},{40,32},{48,40},{56,48},{64,56},{72,6... | collective-permute-start | bytes 884744 | tf_op jit(solution)/shard_map/ppermute | solution.py:17
  293.0 2.7 copy-start
  293.0 64.7 %collective-permute-start.7 = (bf16[128,1152]{1,0:T(8,128)(2,1)S(1)}, bf16[128,1152]{1,0:T(8,128)(2,1)S(1)}, u32[]{:S(2)}, u32[]{:S(2)}) collective-permute-start(bf16[128,1152]{1,0:T(8,128)(2,1)S(1)} %add_convert_fusion), channel_id=1, source_target_pairs={{1008,0},{1016,8},{0,16},{8,24},{16,32},{24,40},{32,48},{40,56},{4... | collective-permute-start | bytes 884744 | tf_op jit(solution)/shard_map/ppermute | solution.py:17
  295.7 225.5 %copy-start.1 = (bf16[128,1152]{1,0:T(8,128)(2,1)S(1)}, bf16[128,1152]{1,0:T(8,128)(2,1)}, u32[]{:S(2)}) copy-start(bf16[128,1152]{1,0:T(8,128)(2,1)} %param.5) | copy-start | bytes 884740
  521.1 1.4 copy-start.3
Sparse Core Ops, SparseCore 0:
  12.9 228.0 all-gather.1
  246.8 274.2 reduce-scatter.1
where the time goes:
time: 531 us; the launch traced here: 530 us
  waiting for transfers between devices  438 us (82%)
  starting transfers between devices  52 us (10%)
  between operations  16.8 us (3%)
  matrix products  12 us (2%)
  other arithmetic  8.36 us (2%)
    all_gather x1, waiting for transfers between devices, on_device(): shard_rows = lax.all_gather(text_unit, 'grp', axis=0, tiled=True)  187 us
    reduce_scatter x1, waiting for transfers between devices, on_device(): lax.psum_scatter(group_grads.astype(jnp.float32).astype(jnp.bfloat16), 'g...  163 us
    ppermute x8, waiting for transfers between devices, passed_along(): return lax.ppermute(block, axis, route)  87.8 us
    ppermute x8, starting transfers between devices, passed_along(): return lax.ppermute(block, axis, route)  52 us
  transfers between devices with their start and end apart: 10, of which 7 were waited for; matrix products, arithmetic and copies ran while one was open for 3% of the time, Pallas kernels for 0%

commit v1 on v0

v1 whole, which is shorter than its diff:
```python
import jax
import jax.numpy as jnp
from jax import lax
from jax.experimental import pallas as pl
from jax.experimental.pallas import tpu as pltpu
from jax.sharding import PartitionSpec as P

MESH = pl.DeviceIdType.MESH

epsilon = 1e-06
logit_scale = 16.0
logit_bias = -2.0

PIECES = 4
STEPS = 2 * PIECES
AHEAD = 3
OWN = 4
FAR = 8


def normalize_rows(emb_ref, mag_ref, unit_ref, first):
    rows = emb_ref.shape[0]

    def some(i, carry):
        at = pl.ds(pl.multiple_of(i * 16, 16), 16)
        values = emb_ref[at, :].astype(jnp.float32)
        magnitude = jnp.sqrt(jnp.sum(values * values, axis=-1, keepdims=True) + epsilon)
        mag_ref[at, :] = magnitude
        unit = (values / magnitude).astype(jnp.bfloat16)
        unit_ref[pl.ds(pl.multiple_of(first + i * 16, 16), 16), :] = unit
        return carry

    lax.fori_loop(0, rows // 16, some, 0)


def backward_rows(emb_ref, mag_ref, sum_ref, out_ref):
    rows = emb_ref.shape[0]

    def some(i, carry):
        at = pl.ds(pl.multiple_of(i * 16, 16), 16)
        magnitude = mag_ref[at, :]
        full = emb_ref[at, :].astype(jnp.float32) / magnitude
        grad = logit_scale * sum_ref[at, :]
        along = jnp.sum(full * grad, axis=-1, keepdims=True)
        out_ref[at, :] = ((grad - full * along) / magnitude).astype(jnp.bfloat16)
        return carry

    lax.fori_loop(0, rows // 16, some, 0)


def kernel(
    image_ref, text_ref, mask_ref, neg_ref,
    loss_ref, image_out, text_out,
    own, held, tiles, image_mag, text_mag, image_sum, text_sum, loss_sum,
    far_send, far_recv, slot_send, slot_recv, tile_send, tile_recv, pass_send, pass_recv,
):
    rows = image_ref.shape[0]
    part = rows // PIECES
    p = lax.axis_index("blk")
    g = lax.axis_index("grp")
    n = lax.axis_size("blk")
    half, y = g // 4, lax.rem(g, 4)
    core = lax.rem(p, 2)

    def near(dy):
        return (p, half * 4 + lax.rem(y + dy, 4))

    far = (p, lax.rem(g + 4, 8))
    after = (lax.rem(p + 2, n), g)
    before = (lax.rem(p + n - 2, n), g)
    twin = (p + 1 - 2 * core, g)
    partners = [far, after, before, twin, near(1), near(2), near(3)]

    barrier = pltpu.get_barrier_semaphore()
    for device in partners:
        pl.semaphore_signal(barrier, inc=1, device_id=device, device_id_type=MESH)

    lane = lax.broadcasted_iota(jnp.int32, (8, 128), 1)
    mine = (lane == neg_ref[0, 0]) | (lane == neg_ref[0, 1]) | (lane == g)
    tile = jnp.where(mine, 1.0, 0.0)
    for k in range(4):
        tile = jnp.where(lane == 8 + k, mask_ref[0, k].astype(jnp.float32), tile)
    tiles[OWN] = tile
    normalize_rows(text_ref, text_mag, own, 0)
    normalize_rows(image_ref, image_mag, own, rows)
    held[OWN] = own[...]
    image_sum[...] = jnp.zeros_like(image_sum)
    text_sum[...] = jnp.zeros_like(text_sum)
    loss_sum[...] = jnp.zeros_like(loss_sum)

    def far_copy(j):
        at = pl.ds(pl.multiple_of(j * part, part), part)
        return pltpu.make_async_remote_copy(
            src_ref=own.at[at], dst_ref=held.at[FAR, at],
            send_sem=far_send.at[j], recv_sem=far_recv.at[j],
            device_id=far, device_id_type=MESH,
        )

    def slot_copy(i, src, slot, device):
        return pltpu.make_async_remote_copy(
            src_ref=src, dst_ref=held.at[slot],
            send_sem=slot_send.at[i], recv_sem=slot_recv.at[slot],
            device_id=device, device_id_type=MESH,
        )

    def tile_copy(i, src_slot, slot, device):
        return pltpu.make_async_remote_copy(
            src_ref=tiles.at[src_slot], dst_ref=tiles.at[slot],
            send_sem=tile_send.at[i], recv_sem=tile_recv.at[slot],
            device_id=device, device_id_type=MESH,
        )

    def pass_copy(dy, j):
        at = pl.ds(pl.multiple_of(j * part, part), part)
        return pltpu.make_async_remote_copy(
            src_ref=held.at[FAR, at], dst_ref=held.at[FAR + 4 - dy, at],
            send_sem=pass_send.at[dy - 1, j], recv_sem=pass_recv.at[3 - dy, j],
            device_id=near(dy), device_id_type=MESH,
        )

    pl.semaphore_wait(barrier, len(partners))

    for j in range(AHEAD):
        far_copy(j).start()
    targets = [(after, 0), (before, 3), (twin, 1 + core)] + [(near(dy), OWN + 4 - dy) for dy in (1, 2, 3)]
    for i, (device, slot) in enumerate(targets):
        tile_copy(i, OWN, slot, device).start()
    tile_copy(6, OWN, FAR, far).start()
    for i, (device, slot) in enumerate(targets):
        slot_copy(i, own, slot, device).start()

    source, place = 3 - 3 * core, 2 - core
    tile_copy(7, source, source, twin).wait_recv()
    tile_copy(7, source, place, twin).start()
    slot_copy(6, held.at[source], source, twin).wait_recv()
    slot_copy(6, held.at[source], place, twin).start()
    tile_copy(6, FAR, FAR, far).wait_recv()
    for dy in (1, 2, 3):
        tile_copy(7 + dy, FAR, FAR + 4 - dy, near(dy)).start()

    row = lax.broadcasted_iota(jnp.int32, (rows, rows), 0)
    column = lax.broadcasted_iota(jnp.int32, (rows, rows), 1)
    eye = jnp.where(row == column, 1.0, 0.0)
    first_lane = lax.broadcasted_iota(jnp.int32, (1, 128), 1)

    def weight(slot, index):
        picked = jnp.where(first_lane == index, tiles[slot, 0:1, :], 0.0)
        return jnp.sum(picked, axis=1, keepdims=True)

    def scores_of(own_block, other):
        return logit_scale * lax.dot_general(
            own_block, other, (((1,), (1,)), ((), ())), preferred_element_type=jnp.float32
        ) + logit_bias

    def image_side(slot, index, diagonal):
        other = held[slot, pl.ds(0, rows), :]
        scores = scores_of(own[pl.ds(rows, rows), :], other)
        w = weight(OWN, index)
        small = jnp.exp(-jnp.abs(scores))
        loss = jnp.maximum(scores, 0.0) + jnp.log1p(small)
        grad = jnp.where(scores >= 0.0, 1.0, small) / (1.0 + small)
        if diagonal is not None:
            loss = loss - diagonal * scores
            grad = grad - diagonal
        loss_sum[...] += w * loss
        image_sum[...] += jnp.dot(
            (w * grad).astype(jnp.bfloat16), other, preferred_element_type=jnp.float32
        )

    def text_side(slot, index, diagonal):
        other = held[slot, pl.ds(rows, rows), :]
        scores = scores_of(own[pl.ds(0, rows), :], other)
        w = weight(slot, index)
        small = jnp.exp(-jnp.abs(scores))
        grad = jnp.where(scores >= 0.0, 1.0, small) / (1.0 + small)
        if diagonal is not None:
            grad = grad - diagonal
        text_sum[...] += jnp.dot(
            (w * grad).astype(jnp.bfloat16), other, preferred_element_type=jnp.float32
        )

    def step(j, carry):
        far_copy(j).wait_recv()
        for dy in (1, 2, 3):
            pass_copy(dy, j).start()
        far_copy(j).wait_send()

        @pl.when(j < STEPS - AHEAD)
        def _():
            far_copy(j + AHEAD).start()

        @pl.when((j != OWN) & (j != source))
        def _():
            slot_copy(0, own, j, after).wait_recv()
            tile_copy(0, OWN, j, after).wait_recv()

        in_loop = j < 4
        group_index = half * 4 + lax.rem(y + j, 4)
        diagonal = jnp.where(j == OWN, 1.0, 0.0) * eye
        image_side(j, jnp.where(in_loop, 8 + j, group_index), diagonal)
        text_side(j, jnp.where(in_loop, 11 - j, g), diagonal)

        @pl.when(j >= 4)
        def _():
            @pl.when(j > 4)
            def _():
                def arrived(k, c):
                    at = pl.ds(pl.multiple_of(k * part, part), part)
                    pltpu.make_async_remote_copy(
                        src_ref=own.at[at], dst_ref=held.at[j + 4, at],
                        send_sem=far_send.at[k], recv_sem=pass_recv.at[j - 5, k],
                        device_id=far, device_id_type=MESH,
                    ).wait_recv()
                    return c
                lax.fori_loop(0, PIECES, arrived, 0)

            image_side(j + 4, (1 - half) * 4 + lax.rem(y + j, 4), None)

        return carry

    lax.fori_loop(0, STEPS, step, 0)
    loss_ref[...] = jnp.sum(loss_sum[...].T, axis=0, keepdims=True)
    backward_rows(image_ref, image_mag, image_sum, image_out)

    def last(r, carry):
        @pl.when(r > 0)
        def _():
            def arrived(k, c):
                at = pl.ds(pl.multiple_of(k * part, part), part)
                pltpu.make_async_remote_copy(
                    src_ref=own.at[at], dst_ref=held.at[FAR + r, at],
                    send_sem=far_send.at[k], recv_sem=pass_recv.at[r - 1, k],
                    device_id=far, device_id_type=MESH,
                ).wait_recv()
                return c
            lax.fori_loop(PIECES, STEPS, arrived, 0)
            tile_copy(0, OWN, FAR + r, after).wait_recv()

        text_side(FAR + r, g, None)
        return carry

    lax.fori_loop(0, 4, last, 0)
    backward_rows(text_ref, text_mag, text_sum, text_out)

    for i, (device, slot) in enumerate(targets):
        tile_copy(i, OWN, slot, device).wait_send()
        slot_copy(i, own, slot, device).wait_send()
    tile_copy(6, OWN, FAR, far).wait_send()
    tile_copy(7, source, place, twin).wait_send()
    slot_copy(6, held.at[source], place, twin).wait_send()
    for dy in (1, 2, 3):
        tile_copy(7 + dy, FAR, FAR + 4 - dy, near(dy)).wait_send()

    def sent(j, carry):
        for dy in (1, 2, 3):
            pass_copy(dy, j).wait_send()
        return carry

    lax.fori_loop(0, STEPS, sent, 0)


def on_device(image_emb, text_emb, loop_mask, neg_list):
    rows, width = image_emb.shape
    vmem = pl.BlockSpec(memory_space=pltpu.VMEM)
    smem = pl.BlockSpec(memory_space=pltpu.SMEM)
    losses, image_grad, text_grad = pl.pallas_call(
        kernel,
        out_shape=(
            jax.ShapeDtypeStruct((1, rows), jnp.float32),
            jax.ShapeDtypeStruct((rows, width), jnp.bfloat16),
            jax.ShapeDtypeStruct((rows, width), jnp.bfloat16),
        ),
        in_specs=[vmem, vmem, smem, smem],
        out_specs=(vmem, vmem, vmem),
        scratch_shapes=[
            pltpu.VMEM((2 * rows, width), jnp.bfloat16),
            pltpu.VMEM((12, 2 * rows, width), jnp.bfloat16),
            pltpu.VMEM((12, 8, 128), jnp.float32),
            pltpu.VMEM((rows, 1), jnp.float32),
            pltpu.VMEM((rows, 1), jnp.float32),
            pltpu.VMEM((rows, width), jnp.float32),
            pltpu.VMEM((rows, width), jnp.float32),
            pltpu.VMEM((rows, rows), jnp.float32),
            pltpu.SemaphoreType.DMA((STEPS,)),
            pltpu.SemaphoreType.DMA((STEPS,)),
            pltpu.SemaphoreType.DMA((7,)),
            pltpu.SemaphoreType.DMA((8,)),
            pltpu.SemaphoreType.DMA((11,)),
            pltpu.SemaphoreType.DMA((12,)),
            pltpu.SemaphoreType.DMA((3, STEPS)),
            pltpu.SemaphoreType.DMA((3, STEPS)),
        ],
        compiler_params=pltpu.CompilerParams(
            collective_id=0, has_side_effects=True, vmem_limit_bytes=32 * 2**20
        ),
        name="pair_blocks",
    )(image_emb, text_emb, loop_mask, neg_list)
    return losses.reshape(rows), image_grad, text_grad


def solution(mesh):
    placed = (
        P(("blk", "grp"), None),
        P(("blk", "grp"), None),
        P(("blk", "grp"), None),
        P(("blk", "grp"), None),
    )
    return jax.shard_map(
        on_device,
        mesh=mesh,
        in_specs=placed,
        out_specs=(P(("blk", "grp")), P(("blk", "grp"), None), P(("blk", "grp"), None)),
        check_vma=False,
    )
```

time: 531 us -> 185 us (0.35)
  waiting for transfers between devices: 438 us -> 0 us
  Pallas kernels: 0 us -> 179 us
  starting transfers between devices: 52 us -> 0 us
  between operations: 16.8 us -> 0.65 us
  matrix products: 12 us -> 0 us
  other arithmetic: 8.36 us -> 0 us
    all_gather x1 -> x0, waiting for transfers between devices: 187 us -> none  [on_device(): shard_rows = lax.all_gather(text_unit, 'grp', axis=0, tiled=True)]
    pallas_call x0 -> x1, Pallas kernels: none -> 179 us  [on_device(): pl.pallas_call(kernel, out_shape=(jax.ShapeDtypeStruct((1, rows), jnp.flo...]
    reduce_scatter x1 -> x0, waiting for transfers between devices: 163 us -> none  [on_device(): lax.psum_scatter(group_grads.astype(jnp.float32).astype(jnp.bfloat16), 'g...]
    ppermute x8 -> x0, waiting for transfers between devices: 87.8 us -> none  [passed_along(): return lax.ppermute(block, axis, route)]
    ppermute x8 -> x0, starting transfers between devices: 52 us -> none  [passed_along(): return lax.ppermute(block, axis, route)]
    dot_general x18 -> x0, matrix products: 12 us -> none  [the longest x6 5.36 us: pair_terms(): lax.dot_general(image_unit, text_block, (((1,), (1,)), ((), ())), preferr...]
  transfers between devices with their start and end apart: 10 -> 0, of which waited for: 7 -> 0; matrix products, arithmetic and copies ran while one was open for 3% -> 0% of each run, Pallas kernels for 0% -> 0%
where the time goes in v1:
time: 185 us
  Pallas kernels  179 us (97%)
  local copies, waits for them, and re-layouts  5.16 us (3%)
    pallas_call x1, Pallas kernels, on_device(): pl.pallas_call(kernel, out_shape=(jax.ShapeDtypeStruct((1, rows), jnp.flo...  179 us
    unnamed x11, local copies, waits for them, and re-layouts  5.16 us

profile of v1, /device:TPU:1, one launch (start us, length us, event | category | flops | bytes accessed | tf_op | source)
XLA Modules:
  0.0 185.0 jit_solution(13689611014693127558)
XLA Ops:
  0.6 0.0 copy-start
  0.6 1.0 copy-done
  1.6 0.0 copy-start.1
  1.6 1.0 copy-done.1
  2.6 0.0 copy-start.2
  2.6 0.7 copy-done.2
  3.2 0.0 copy-start.3
  3.2 0.7 copy-done.3
  3.9 179.2 %pair_blocks.1 = (f32[1,128]{1,0:T(1,128)S(1)}, bf16[128,1152]{1,0:T(8,128)(2,1)S(1)}, bf16[128,1152]{1,0:T(8,128)(2,1)S(1)}) custom-call(bf16[128,1152]{1,0:T(8,128)(2,1)S(1)} %copy-done, bf16[128,1152]{1,0:T(8,128)(2,1)S(1)} %copy-done.1, s32[1,4]{1,0:T(1,128)S(1)} %copy-done.2, s32[1,2]{1,0:T(1,128)S(1)} %copy-done.3), custom_call_target="tpu_custom_call" | custom-call | tf_op jit(solution)/shard_map/pair_blocks/pallas_call | solution.py:266
  183.1 0.5 copy.10
  183.6 0.7 copy.11
  184.3 0.7 copy.12
Async XLA Ops:
  0.6 1.0 copy-start
  1.6 1.0 copy-start.1
  2.6 0.7 copy-start.2
  3.2 0.7 copy-start.3

commit v2 on v1

v2 whole, which is shorter than its diff:
```python
import jax
import jax.numpy as jnp
from jax import lax
from jax.experimental import pallas as pl
from jax.experimental.pallas import tpu as pltpu
from jax.sharding import PartitionSpec as P

MESH = pl.DeviceIdType.MESH

epsilon = 1e-06
logit_scale = 16.0
logit_bias = -2.0

PIECES = 4
LAG = 1
OWN = 4
FAR = 8


def normalize_rows(emb_ref, mag_ref, unit_ref, first):
    rows = emb_ref.shape[0]

    def some(i, carry):
        at = pl.ds(pl.multiple_of(i * 16, 16), 16)
        values = emb_ref[at, :].astype(jnp.float32)
        magnitude = jnp.sqrt(jnp.sum(values * values, axis=-1, keepdims=True) + epsilon)
        mag_ref[at, :] = magnitude
        unit = (values / magnitude).astype(jnp.bfloat16)
        unit_ref[pl.ds(pl.multiple_of(first + i * 16, 16), 16), :] = unit
        return carry

    lax.fori_loop(0, rows // 16, some, 0)


def backward_rows(emb_ref, mag_ref, sum_ref, more_ref, out_ref, first, count):
    def some(i, carry):
        at = pl.ds(pl.multiple_of(first + i * 16, 16), 16)
        magnitude = mag_ref[at, :]
        full = emb_ref[at, :].astype(jnp.float32) / magnitude
        grad = sum_ref[at, :]
        if more_ref is not None:
            grad = grad + more_ref[at, :].astype(jnp.float32)
        grad = logit_scale * grad
        along = jnp.sum(full * grad, axis=-1, keepdims=True)
        out_ref[at, :] = ((grad - full * along) / magnitude).astype(jnp.bfloat16)
        return carry

    lax.fori_loop(0, count // 16, some, 0)


def kernel(
    image_hbm, text_hbm, mask_ref, neg_ref,
    loss_ref, image_out, text_out,
    image_ref, text_ref, own, held, tiles, image_mag, text_mag, image_sum, text_sum, loss_sum,
    far_weight, sent_back, got_back,
    load_sem, far_send, far_recv, slot_send, slot_recv, tile_send, tile_recv, pass_send, pass_recv,
    back_send, back_recv,
):
    rows = image_ref.shape[0]
    part = rows // PIECES
    p = lax.axis_index("blk")
    g = lax.axis_index("grp")
    n = lax.axis_size("blk")
    half, y = g // 4, lax.rem(g, 4)
    core = lax.rem(p, 2)
    low, high = p < 2, p >= n - 2
    closing = low | high

    def near(dy):
        return (p, half * 4 + lax.rem(y + dy, 4))

    other_half = lax.rem(g + 4, 8)
    far = (p, other_half)
    next_p, last_p = lax.rem(p + 2, n), lax.rem(p + n - 2, n)
    after, before = (next_p, g), (last_p, g)
    twin = (p + 1 - 2 * core, g)
    partners = [far, after, before, twin, near(1), near(2), near(3)]

    barrier = pltpu.get_barrier_semaphore()
    for device in partners:
        pl.semaphore_signal(barrier, inc=1, device_id=device, device_id_type=MESH)

    load_text = pltpu.make_async_copy(text_hbm, text_ref, load_sem.at[0])
    load_image = pltpu.make_async_copy(image_hbm, image_ref, load_sem.at[1])
    load_text.start()
    load_image.start()

    lane = lax.broadcasted_iota(jnp.int32, (8, 128), 1)
    mine = (lane == neg_ref[0, 0]) | (lane == neg_ref[0, 1]) | (lane == g)
    tile = jnp.where(mine, 1.0, 0.0)
    for k in range(4):
        tile = jnp.where(lane == 8 + k, mask_ref[0, k].astype(jnp.float32), tile)
    tiles[OWN] = tile
    load_text.wait()
    normalize_rows(text_ref, text_mag, own, 0)

    def slot_rows(slot):
        return pl.ds(pl.multiple_of(slot * (2 * rows), 2 * rows), 2 * rows)

    def piece(j, source):
        return pl.ds(pl.multiple_of(FAR * 2 * rows + j * (4 * part) + source * part, part), part)

    def far_copy(j):
        at = pl.ds(pl.multiple_of(j * part, part), part)
        return pltpu.make_async_remote_copy(
            src_ref=own.at[at], dst_ref=held.at[piece(j, 0)],
            send_sem=far_send.at[j], recv_sem=far_recv.at[j],
            device_id=far, device_id_type=MESH,
        )

    def slot_copy(i, src, slot, device):
        return pltpu.make_async_remote_copy(
            src_ref=src, dst_ref=held.at[slot_rows(slot)],
            send_sem=slot_send.at[i], recv_sem=slot_recv.at[slot],
            device_id=device, device_id_type=MESH,
        )

    def tile_copy(i, src_slot, slot, device):
        return pltpu.make_async_remote_copy(
            src_ref=tiles.at[src_slot], dst_ref=tiles.at[slot],
            send_sem=tile_send.at[i], recv_sem=tile_recv.at[slot],
            device_id=device, device_id_type=MESH,
        )

    def pass_copy(dy, j):
        return pltpu.make_async_remote_copy(
            src_ref=held.at[piece(j, 0)], dst_ref=held.at[piece(j, 4 - dy)],
            send_sem=pass_send.at[dy - 1, j], recv_sem=pass_recv.at[3 - dy, j],
            device_id=near(dy), device_id_type=MESH,
        )

    def back_copy(j):
        at = pl.ds(pl.multiple_of(j * part, part), part)
        return pltpu.make_async_remote_copy(
            src_ref=sent_back.at[at], dst_ref=got_back.at[at],
            send_sem=back_send.at[j], recv_sem=back_recv.at[j],
            device_id=far, device_id_type=MESH,
        )

    pl.semaphore_wait(barrier, len(partners))

    def send_far(j, carry):
        far_copy(j).start()
        return carry

    lax.fori_loop(0, PIECES, send_far, 0)
    load_image.wait()
    normalize_rows(image_ref, image_mag, own, rows)

    targets = [(after, 0), (before, 3), (twin, 1 + core)] + [(near(dy), OWN + 4 - dy) for dy in (1, 2, 3)]
    for i, (device, slot) in enumerate(targets):
        tile_copy(i, OWN, slot, device).start()
    for i in (3, 4, 5, 2, 0, 1):
        device, slot = targets[i]
        slot_copy(i, own, slot, device).start()

    held[slot_rows(OWN), :] = own[...]
    image_sum[...] = jnp.zeros_like(image_sum)
    text_sum[...] = jnp.zeros_like(text_sum)
    loss_sum[...] = jnp.zeros_like(loss_sum)

    source, place = 3 - 3 * core, 2 - core
    late = (low & (core == 1)) | (high & (core == 0))

    row = lax.broadcasted_iota(jnp.int32, (rows, rows), 0)
    column = lax.broadcasted_iota(jnp.int32, (rows, rows), 1)
    eye = jnp.where(row == column, 1.0, 0.0)
    first_lane = lax.broadcasted_iota(jnp.int32, (1, 128), 1)

    def weight(slot, index):
        picked = jnp.where(first_lane == index, tiles[slot, 0:1, :], 0.0)
        return jnp.sum(picked, axis=1, keepdims=True)

    def scores_of(own_block, other):
        return logit_scale * lax.dot_general(
            own_block, other, (((1,), (1,)), ((), ())), preferred_element_type=jnp.float32
        ) + logit_bias

    def sigmoid_of(scores):
        small = jnp.exp(-jnp.abs(scores))
        return jnp.where(scores >= 0.0, 1.0, small) / (1.0 + small)

    def image_side(other, w, diagonal):
        scores = scores_of(own[pl.ds(rows, rows), :], other)
        small = jnp.exp(-jnp.abs(scores))
        loss = jnp.maximum(scores, 0.0) + jnp.log1p(small)
        grad = jnp.where(scores >= 0.0, 1.0, small) / (1.0 + small)
        if diagonal is not None:
            loss = loss - diagonal * scores
            grad = grad - diagonal
        loss_sum[...] += w * loss
        image_sum[...] += jnp.dot(
            (w * grad).astype(jnp.bfloat16), other, preferred_element_type=jnp.float32
        )

    def text_side(other, w, diagonal):
        scores = scores_of(own[pl.ds(0, rows), :], other)
        text_sum[...] += jnp.dot(
            (w * (sigmoid_of(scores) - diagonal)).astype(jnp.bfloat16), other, preferred_element_type=jnp.float32
        )

    def unit(slot):
        in_loop = slot < 4
        group_index = half * 4 + lax.rem(y + slot, 4)
        diagonal = jnp.where(slot == OWN, 1.0, 0.0) * eye
        first = pl.multiple_of(slot * (2 * rows), 2 * rows)
        w = weight(OWN, jnp.where(in_loop, 8 + slot, group_index))
        image_side(held[pl.ds(first, rows), :], w, diagonal)
        w = weight(slot, jnp.where(in_loop, 11 - slot, g))
        text_side(held[pl.ds(first + rows, rows), :], w, diagonal)

    def far_weights():
        w = jnp.zeros((1, 128), jnp.float32)
        for r in range(4):
            w = jnp.where(first_lane // part == r, weight(OWN, (1 - half) * 4 + lax.rem(y + r, 4)), w)
            far_weight[r] = jnp.broadcast_to(weight(OWN + r, other_half), (8, 128))
        far_weight[4] = jnp.broadcast_to(w, (8, 128))

    def far_piece(k):
        first = pl.multiple_of(FAR * 2 * rows + k * (4 * part), 4 * part)
        return held[pl.ds(first, 4 * part), :]

    def arrived(k):
        for dy in (1, 2, 3):
            pass_copy(dy, k).wait_recv()

    def relay():
        slot_copy(6, held.at[slot_rows(source)], source, twin).wait_recv()
        slot_copy(6, held.at[slot_rows(source)], place, twin).start()
        tile_copy(6, source, source, twin).wait_recv()
        tile_copy(6, source, place, twin).start()

    def units(slot, carry):
        @pl.when((slot != OWN) & (slot != source))
        def _():
            slot_copy(0, own, slot, after).wait_recv()
            tile_copy(0, OWN, slot, after).wait_recv()

        unit(slot)
        return carry

    @pl.when(jnp.logical_not(late))
    def _():
        relay()

    lax.fori_loop(OWN, OWN + 4, units, 0)
    far_weights()

    @pl.when(jnp.logical_not(closing))
    def _():
        lax.fori_loop(0, 4, units, 0)

    def step(j, carry):
        far_copy(j).wait_recv()
        for dy in (1, 2, 3):
            pass_copy(dy, j).start()

        text_piece = held[piece(j, 0), :]
        total = jnp.zeros((part, image_ref.shape[1]), jnp.float32)
        for r in range(4):
            images = held[pl.ds((OWN + r) * 2 * rows + rows, rows), :]
            scores = scores_of(text_piece, images)
            grad = far_weight[r, 0:1, :] * sigmoid_of(scores)
            total += jnp.dot(grad.astype(jnp.bfloat16), images, preferred_element_type=jnp.float32)
        sent_back[pl.ds(pl.multiple_of(j * part, part), part), :] = total.astype(jnp.bfloat16)
        back_copy(j).start()

        @pl.when(j >= LAG)
        def _():
            far_image(j - LAG)

        return carry

    def far_image(k):
        arrived(k)
        image_side(far_piece(k), far_weight[4, 0:1, :], None)

    lax.fori_loop(0, PIECES, step, 0)

    @pl.when(closing)
    def _():
        @pl.when(late)
        def _():
            relay()

        lax.fori_loop(0, 4, units, 0)

    for k in range(PIECES - LAG, PIECES):
        far_image(k)
    loss_ref[...] = jnp.sum(loss_sum[...].T, axis=0, keepdims=True)
    backward_rows(image_ref, image_mag, image_sum, None, image_out, 0, rows)

    def finish(j, carry):
        back_copy(j).wait_recv()
        backward_rows(text_ref, text_mag, text_sum, got_back, text_out, j * part, part)
        return carry

    lax.fori_loop(0, PIECES, finish, 0)

    for i, (device, slot) in enumerate(targets):
        tile_copy(i, OWN, slot, device).wait_send()
        slot_copy(i, own, slot, device).wait_send()
    tile_copy(6, source, place, twin).wait_send()
    slot_copy(6, held.at[slot_rows(source)], place, twin).wait_send()

    def sent(j, carry):
        for dy in (1, 2, 3):
            pass_copy(dy, j).wait_send()
        far_copy(j).wait_send()
        back_copy(j).wait_send()
        return carry

    lax.fori_loop(0, PIECES, sent, 0)


def on_device(image_emb, text_emb, loop_mask, neg_list):
    rows, width = image_emb.shape
    vmem = pl.BlockSpec(memory_space=pltpu.VMEM)
    hbm = pl.BlockSpec(memory_space=pl.ANY)
    smem = pl.BlockSpec(memory_space=pltpu.SMEM)
    losses, image_grad, text_grad = pl.pallas_call(
        kernel,
        out_shape=(
            jax.ShapeDtypeStruct((1, rows), jnp.float32),
            jax.ShapeDtypeStruct((rows, width), jnp.bfloat16),
            jax.ShapeDtypeStruct((rows, width), jnp.bfloat16),
        ),
        in_specs=[hbm, hbm, smem, smem],
        out_specs=(vmem, vmem, vmem),
        scratch_shapes=[
            pltpu.VMEM((rows, width), jnp.bfloat16),
            pltpu.VMEM((rows, width), jnp.bfloat16),
            pltpu.VMEM((2 * rows, width), jnp.bfloat16),
            pltpu.VMEM((FAR * 2 * rows + 4 * rows, width), jnp.bfloat16),
            pltpu.VMEM((8, 8, 128), jnp.float32),
            pltpu.VMEM((rows, 1), jnp.float32),
            pltpu.VMEM((rows, 1), jnp.float32),
            pltpu.VMEM((rows, width), jnp.float32),
            pltpu.VMEM((rows, width), jnp.float32),
            pltpu.VMEM((rows, rows), jnp.float32),
            pltpu.VMEM((5, 8, 128), jnp.float32),
            pltpu.VMEM((rows, width), jnp.bfloat16),
            pltpu.VMEM((rows, width), jnp.bfloat16),
            pltpu.SemaphoreType.DMA((2,)),
            pltpu.SemaphoreType.DMA((PIECES,)),
            pltpu.SemaphoreType.DMA((PIECES,)),
            pltpu.SemaphoreType.DMA((7,)),
            pltpu.SemaphoreType.DMA((8,)),
            pltpu.SemaphoreType.DMA((7,)),
            pltpu.SemaphoreType.DMA((8,)),
            pltpu.SemaphoreType.DMA((3, PIECES)),
            pltpu.SemaphoreType.DMA((3, PIECES)),
            pltpu.SemaphoreType.DMA((PIECES,)),
            pltpu.SemaphoreType.DMA((PIECES,)),
        ],
        compiler_params=pltpu.CompilerParams(
            collective_id=0, has_side_effects=True, vmem_limit_bytes=32 * 2**20
        ),
        name="pair_blocks",
    )(image_emb, text_emb, loop_mask, neg_list)
    return losses.reshape(rows), image_grad, text_grad


def solution(mesh):
    placed = (
        P(("blk", "grp"), None),
        P(("blk", "grp"), None),
        P(("blk", "grp"), None),
        P(("blk", "grp"), None),
    )
    return jax.shard_map(
        on_device,
        mesh=mesh,
        in_specs=placed,
        out_specs=(P(("blk", "grp")), P(("blk", "grp"), None), P(("blk", "grp"), None)),
        check_vma=False,
    )
```

time: 185 us -> 166 us (0.90)
  the two profiles are of different devices: /device:TPU:1 before, /device:TPU:63 now
where the time goes in v2:
time: 166 us
  Pallas kernels  160 us (96%)
  local copies, waits for them, and re-layouts  5.16 us (3%)
    pallas_call x1, Pallas kernels, on_device(): pl.pallas_call(kernel, out_shape=(jax.ShapeDtypeStruct((1, rows), jnp.flo...  160 us
    unnamed x11, local copies, waits for them, and re-layouts  5.16 us

profile of v2, /device:TPU:63, one launch (start us, length us, event | category | flops | bytes accessed | tf_op | source)
XLA Modules:
  0.0 165.9 jit_solution(2783152170659272207)
XLA Ops:
  0.6 0.0 copy-start
  0.6 1.0 copy-done
  1.6 0.0 copy-start.1
  1.6 1.0 copy-done.1
  2.6 0.0 copy-start.2
  2.6 0.7 copy-done.2
  3.2 0.0 copy-start.3
  3.2 0.7 copy-done.3
  3.9 160.1 %pair_blocks.1 = (f32[1,128]{1,0:T(1,128)S(1)}, bf16[128,1152]{1,0:T(8,128)(2,1)S(1)}, bf16[128,1152]{1,0:T(8,128)(2,1)S(1)}) custom-call(bf16[128,1152]{1,0:T(8,128)(2,1)S(1)} %copy-done, bf16[128,1152]{1,0:T(8,128)(2,1)S(1)} %copy-done.1, s32[1,4]{1,0:T(1,128)S(1)} %copy-done.2, s32[1,2]{1,0:T(1,128)S(1)} %copy-done.3), custom_call_target="tpu_custom_call" | custom-call | tf_op jit(solution)/shard_map/pair_blocks/pallas_call | solution.py:321
  164.0 0.5 copy.10
  164.5 0.7 copy.11
  165.2 0.7 copy.12
Async XLA Ops:
  0.6 1.0 copy-start
  1.6 1.0 copy-start.1
  2.6 0.7 copy-start.2
  3.2 0.7 copy-start.3

commit v3 on v2

--- a/solution.py
+++ b/solution.py
@@ -12,6 +12,7 @@
 logit_bias = -2.0
 
 PIECES = 4
+BITS = 2 * PIECES
 LAG = 1
 OWN = 4
 FAR = 8
@@ -29,7 +30,7 @@
         unit_ref[pl.ds(pl.multiple_of(first + i * 16, 16), 16), :] = unit
         return carry
 
-    lax.fori_loop(0, rows // 16, some, 0)
+    lax.fori_loop(0, rows // 16, some, 0, unroll=4)
 
 
 def backward_rows(emb_ref, mag_ref, sum_ref, more_ref, out_ref, first, count):
@@ -45,16 +46,16 @@
         out_ref[at, :] = ((grad - full * along) / magnitude).astype(jnp.bfloat16)
         return carry
 
-    lax.fori_loop(0, count // 16, some, 0)
+    lax.fori_loop(0, count // 16, some, 0, unroll=2)
 
 
 def kernel(
-    image_hbm, text_hbm, mask_ref, neg_ref,
+    image_hbm, text_hbm, mask_hbm, neg_hbm,
     loss_ref, image_out, text_out,
-    image_ref, text_ref, own, held, tiles, image_mag, text_mag, image_sum, text_sum, loss_sum,
-    far_weight, sent_back, got_back,
+    image_ref, text_ref, mask_ref, neg_ref, own, held, tiles, image_mag, text_mag, image_sum, text_sum, loss_sum,
+    far_weight, sent_back, got_back, detour,
     load_sem, far_send, far_recv, slot_send, slot_recv, tile_send, tile_recv, pass_send, pass_recv,
-    back_send, back_recv,
+    back_send, back_recv, detour_send, detour_recv,
 ):
     rows = image_ref.shape[0]
     part = rows // PIECES
@@ -63,8 +64,10 @@
     n = lax.axis_size("blk")
     half, y = g // 4, lax.rem(g, 4)
     core = lax.rem(p, 2)
-    low, high = p < 2, p >= n - 2
-    closing = low | high
+    x = lax.rem(p // 2, 4)
+    low, high = x == 0, x == 3
+    turning = low | high
+    beside = p + 2 - 4 * lax.rem(x, 2)
 
     def near(dy):
         return (p, half * 4 + lax.rem(y + dy, 4))
@@ -74,7 +77,7 @@
     next_p, last_p = lax.rem(p + 2, n), lax.rem(p + n - 2, n)
     after, before = (next_p, g), (last_p, g)
     twin = (p + 1 - 2 * core, g)
-    partners = [far, after, before, twin, near(1), near(2), near(3)]
+    partners = [far, (beside, other_half), after, before, twin, near(1), near(2), near(3)]
 
     barrier = pltpu.get_barrier_semaphore()
     for device in partners:
@@ -82,17 +85,21 @@
 
     load_text = pltpu.make_async_copy(text_hbm, text_ref, load_sem.at[0])
     load_image = pltpu.make_async_copy(image_hbm, image_ref, load_sem.at[1])
-    load_text.start()
-    load_image.start()
-
+    load_mask = pltpu.make_async_copy(mask_hbm, mask_ref, load_sem.at[2])
+    load_neg = pltpu.make_async_copy(neg_hbm, neg_ref, load_sem.at[3])
+    loads = [load_text, load_image, load_mask, load_neg]
+    for load in loads:
+        load.start()
+    load_text.wait()
+    normalize_rows(text_ref, text_mag, own, 0)
+    load_mask.wait()
+    load_neg.wait()
     lane = lax.broadcasted_iota(jnp.int32, (8, 128), 1)
     mine = (lane == neg_ref[0, 0]) | (lane == neg_ref[0, 1]) | (lane == g)
     tile = jnp.where(mine, 1.0, 0.0)
     for k in range(4):
         tile = jnp.where(lane == 8 + k, mask_ref[0, k].astype(jnp.float32), tile)
     tiles[OWN] = tile
-    load_text.wait()
-    normalize_rows(text_ref, text_mag, own, 0)
 
     def slot_rows(slot):
         return pl.ds(pl.multiple_of(slot * (2 * rows), 2 * rows), 2 * rows)
@@ -100,13 +107,29 @@
     def piece(j, source):
         return pl.ds(pl.multiple_of(FAR * 2 * rows + j * (4 * part) + source * part, part), part)
 
-    def far_copy(j):
-        at = pl.ds(pl.multiple_of(j * part, part), part)
+    bit = part // 2
+
+    def landing(i):
+        first = FAR * 2 * rows + i // 2 * (4 * part) + lax.rem(i, 2) * bit
+        return pl.ds(pl.multiple_of(first, bit), bit)
+
+    def far_copy(i):
         return pltpu.make_async_remote_copy(
-            src_ref=own.at[at], dst_ref=held.at[piece(j, 0)],
-            send_sem=far_send.at[j], recv_sem=far_recv.at[j],
+            src_ref=own.at[pl.ds(pl.multiple_of(i * bit, bit), bit)], dst_ref=held.at[landing(i)],
+            send_sem=far_send.at[i], recv_sem=far_recv.at[i],
             device_id=far, device_id_type=MESH,
         )
+
+    out_copy = pltpu.make_async_remote_copy(
+        src_ref=own.at[pl.ds((BITS - 1) * bit, bit)], dst_ref=detour,
+        send_sem=far_send.at[BITS - 1], recv_sem=detour_recv,
+        device_id=(beside, other_half), device_id_type=MESH,
+    )
+    in_copy = pltpu.make_async_remote_copy(
+        src_ref=detour, dst_ref=held.at[landing(BITS - 1)],
+        send_sem=detour_send, recv_sem=far_recv.at[BITS - 1],
+        device_id=(beside, g), device_id_type=MESH,
+    )
 
     def slot_copy(i, src, slot, device):
         return pltpu.make_async_remote_copy(
@@ -143,10 +166,19 @@
         far_copy(j).start()
         return carry
 
-    lax.fori_loop(0, PIECES, send_far, 0)
+
+    @pl.when(turning)
+    def _():
+        out_copy.start()
+
+    lax.fori_loop(0, BITS - 1, send_far, 0)
+
+    @pl.when(jnp.logical_not(turning))
+    def _():
+        far_copy(BITS - 1).start()
+
     load_image.wait()
     normalize_rows(image_ref, image_mag, own, rows)
-
     targets = [(after, 0), (before, 3), (twin, 1 + core)] + [(near(dy), OWN + 4 - dy) for dy in (1, 2, 3)]
     for i, (device, slot) in enumerate(targets):
         tile_copy(i, OWN, slot, device).start()
@@ -246,12 +278,18 @@
     lax.fori_loop(OWN, OWN + 4, units, 0)
     far_weights()
 
-    @pl.when(jnp.logical_not(closing))
+    @pl.when(jnp.logical_not(turning))
     def _():
         lax.fori_loop(0, 4, units, 0)
 
     def step(j, carry):
-        far_copy(j).wait_recv()
+        @pl.when((j == PIECES - 2) & jnp.logical_not(turning))
+        def _():
+            out_copy.wait_recv()
+            in_copy.start()
+
+        far_copy(2 * j).wait_recv()
+        far_copy(2 * j + 1).wait_recv()
         for dy in (1, 2, 3):
             pass_copy(dy, j).start()
 
@@ -277,7 +315,7 @@
 
     lax.fori_loop(0, PIECES, step, 0)
 
-    @pl.when(closing)
+    @pl.when(turning)
     def _():
         @pl.when(late)
         def _():
@@ -306,18 +344,22 @@
     def sent(j, carry):
         for dy in (1, 2, 3):
             pass_copy(dy, j).wait_send()
-        far_copy(j).wait_send()
+        far_copy(2 * j).wait_send()
+        far_copy(2 * j + 1).wait_send()
         back_copy(j).wait_send()
         return carry
 
     lax.fori_loop(0, PIECES, sent, 0)
+
+    @pl.when(jnp.logical_not(turning))
+    def _():
+        in_copy.wait_send()
 
 
 def on_device(image_emb, text_emb, loop_mask, neg_list):
     rows, width = image_emb.shape
     vmem = pl.BlockSpec(memory_space=pltpu.VMEM)
-    hbm = pl.BlockSpec(memory_space=pl.ANY)
-    smem = pl.BlockSpec(memory_space=pltpu.SMEM)
+    hbm = pl.BlockSpec(memory_space=pltpu.HBM)
     losses, image_grad, text_grad = pl.pallas_call(
         kernel,
         out_shape=(
@@ -325,11 +367,13 @@
             jax.ShapeDtypeStruct((rows, width), jnp.bfloat16),
             jax.ShapeDtypeStruct((rows, width), jnp.bfloat16),
         ),
-        in_specs=[hbm, hbm, smem, smem],
+        in_specs=[hbm] * 4,
         out_specs=(vmem, vmem, vmem),
         scratch_shapes=[
             pltpu.VMEM((rows, width), jnp.bfloat16),
             pltpu.VMEM((rows, width), jnp.bfloat16),
+            pltpu.SMEM(loop_mask.shape, jnp.int32),
+            pltpu.SMEM(neg_list.shape, jnp.int32),
             pltpu.VMEM((2 * rows, width), jnp.bfloat16),
             pltpu.VMEM((FAR * 2 * rows + 4 * rows, width), jnp.bfloat16),
             pltpu.VMEM((8, 8, 128), jnp.float32),
@@ -341,9 +385,10 @@
             pltpu.VMEM((5, 8, 128), jnp.float32),
             pltpu.VMEM((rows, width), jnp.bfloat16),
             pltpu.VMEM((rows, width), jnp.bfloat16),
-            pltpu.SemaphoreType.DMA((2,)),
-            pltpu.SemaphoreType.DMA((PIECES,)),
-            pltpu.SemaphoreType.DMA((PIECES,)),
+            pltpu.VMEM((rows // BITS, width), jnp.bfloat16),
+            pltpu.SemaphoreType.DMA((4,)),
+            pltpu.SemaphoreType.DMA((BITS,)),
+            pltpu.SemaphoreType.DMA((BITS,)),
             pltpu.SemaphoreType.DMA((7,)),
             pltpu.SemaphoreType.DMA((8,)),
             pltpu.SemaphoreType.DMA((7,)),
@@ -352,9 +397,11 @@
             pltpu.SemaphoreType.DMA((3, PIECES)),
             pltpu.SemaphoreType.DMA((PIECES,)),
             pltpu.SemaphoreType.DMA((PIECES,)),
+            pltpu.SemaphoreType.DMA,
+            pltpu.SemaphoreType.DMA,
         ],
         compiler_params=pltpu.CompilerParams(
-            collective_id=0, has_side_effects=True, vmem_limit_bytes=32 * 2**20
+            collective_id=0, has_side_effects=True, vmem_limit_bytes=60 * 2**20
         ),
         name="pair_blocks",
     )(image_emb, text_emb, loop_mask, neg_list)

time: 166 us -> 155 us (0.934)
  the two profiles are of different devices: /device:TPU:63 before, /device:TPU:1 now
where the time goes in v3:
time: 155 us; the launch traced here: 154 us
  Pallas kernels  150 us (97%)
  local copies, waits for them, and re-layouts  3.56 us (2%)
    pallas_call x1, Pallas kernels, on_device(): pl.pallas_call(kernel, out_shape=(jax.ShapeDtypeStruct((1, rows), jnp.flo...  150 us
    unnamed x7, local copies, waits for them, and re-layouts  3.56 us

profile of v3, /device:TPU:1, one launch (start us, length us, event | category | flops | bytes accessed | tf_op | source)
XLA Modules:
  0.0 153.8 jit_solution(9156584280783108086)
XLA Ops:
  0.6 149.6 %pair_blocks.1 = (f32[1,128]{1,0:T(1,128)}, bf16[128,1152]{1,0:T(8,128)(2,1)}, bf16[128,1152]{1,0:T(8,128)(2,1)}) custom-call(bf16[128,1152]{1,0:T(8,128)(2,1)} %image_hbm.1, bf16[128,1152]{1,0:T(8,128)(2,1)} %text_hbm.1, s32[1,4]{1,0:T(1,128)} %mask_hbm.1, s32[1,2]{1,0:T(1,128)} %neg_hbm.1), custom_call_target="tpu_custom_call" | custom-call | tf_op jit(solution)/shard_map/pair_blocks/pallas_call | solution.py:363
  150.2 0.0 copy-start.1
  150.2 0.6 copy-done.1
  150.8 0.5 copy.10
  151.3 0.0 copy-start
  151.3 1.7 %copy.11 = bf16[128,1152]{1,0:T(8,128)(2,1)} copy(bf16[128,1152]{1,0:T(8,128)(2,1)} %get-tuple-element.13) | data formatting | bytes 589824
  153.0 0.0 copy-done
  153.0 0.7 copy.12
Async XLA Ops:
  150.2 0.6 copy-start.1
  151.3 1.7 %copy-start = (bf16[128,1152]{1,0:T(8,128)(2,1)S(1)}, bf16[128,1152]{1,0:T(8,128)(2,1)}, u32[]{:S(2)}) copy-start(bf16[128,1152]{1,0:T(8,128)(2,1)} %get-tuple-element.14) | copy-start | bytes 884740

commit v4 on v3

--- a/solution.py
+++ b/solution.py
@@ -53,9 +53,9 @@
     image_hbm, text_hbm, mask_hbm, neg_hbm,
     loss_ref, image_out, text_out,
     image_ref, text_ref, mask_ref, neg_ref, own, held, tiles, image_mag, text_mag, image_sum, text_sum, loss_sum,
-    far_weight, sent_back, got_back, detour,
+    far_weight, sent_back, got_back,
     load_sem, far_send, far_recv, slot_send, slot_recv, tile_send, tile_recv, pass_send, pass_recv,
-    back_send, back_recv, detour_send, detour_recv,
+    back_send, back_recv, edge_send, edge_recv, around_send, around_recv,
 ):
     rows = image_ref.shape[0]
     part = rows // PIECES
@@ -67,7 +67,8 @@
     x = lax.rem(p // 2, 4)
     low, high = x == 0, x == 3
     turning = low | high
-    beside = p + 2 - 4 * lax.rem(x, 2)
+    level, levels = p // 8, n // 8
+    ahead = (high & (level < levels - 2)) | (low & (level > 0) & (level < levels - 1))
 
     def near(dy):
         return (p, half * 4 + lax.rem(y + dy, 4))
@@ -77,11 +78,20 @@
     next_p, last_p = lax.rem(p + 2, n), lax.rem(p + n - 2, n)
     after, before = (next_p, g), (last_p, g)
     twin = (p + 1 - 2 * core, g)
-    partners = [far, (beside, other_half), after, before, twin, near(1), near(2), near(3)]
+    closing_low, closing_high = low & (level == 0), high & (level == levels - 1)
+    closing = closing_low | closing_high
+    around = (jnp.where(low, last_p, next_p), other_half)
+    across = (jnp.where(low, last_p, next_p), g)
+    there = jnp.where(low, 3, 0)
+    partners = [far, after, before, twin, near(1), near(2), near(3)]
 
     barrier = pltpu.get_barrier_semaphore()
     for device in partners:
         pl.semaphore_signal(barrier, inc=1, device_id=device, device_id_type=MESH)
+
+    @pl.when(closing)
+    def _():
+        pl.semaphore_signal(barrier, inc=1, device_id=around, device_id_type=MESH)
 
     load_text = pltpu.make_async_copy(text_hbm, text_ref, load_sem.at[0])
     load_image = pltpu.make_async_copy(image_hbm, image_ref, load_sem.at[1])
@@ -120,17 +130,6 @@
             device_id=far, device_id_type=MESH,
         )
 
-    out_copy = pltpu.make_async_remote_copy(
-        src_ref=own.at[pl.ds((BITS - 1) * bit, bit)], dst_ref=detour,
-        send_sem=far_send.at[BITS - 1], recv_sem=detour_recv,
-        device_id=(beside, other_half), device_id_type=MESH,
-    )
-    in_copy = pltpu.make_async_remote_copy(
-        src_ref=detour, dst_ref=held.at[landing(BITS - 1)],
-        send_sem=detour_send, recv_sem=far_recv.at[BITS - 1],
-        device_id=(beside, g), device_id_type=MESH,
-    )
-
     def slot_copy(i, src, slot, device):
         return pltpu.make_async_remote_copy(
             src_ref=src, dst_ref=held.at[slot_rows(slot)],
@@ -160,31 +159,77 @@
             device_id=far, device_id_type=MESH,
         )
 
-    pl.semaphore_wait(barrier, len(partners))
+    def edge_copy():
+        first = pl.multiple_of(there * (2 * rows) + rows, rows)
+        return pltpu.make_async_remote_copy(
+            src_ref=own.at[pl.ds(rows, rows)], dst_ref=held.at[pl.ds(first, rows)],
+            send_sem=edge_send, recv_sem=edge_recv,
+            device_id=across, device_id_type=MESH,
+        )
+
+    def around_copy(j):
+        first = pl.multiple_of(there * (2 * rows) + j * part, part)
+        return pltpu.make_async_remote_copy(
+            src_ref=held.at[piece(j, 0)], dst_ref=held.at[pl.ds(first, part)],
+            send_sem=around_send.at[j], recv_sem=around_recv.at[j],
+            device_id=around, device_id_type=MESH,
+        )
+
+    def closed():
+        edge_copy().wait_recv()
+
+        def came(j, carry):
+            around_copy(j).wait_recv()
+            return carry
+
+        lax.fori_loop(0, PIECES, came, 0)
+
+    pl.semaphore_wait(barrier, len(partners) + jnp.where(closing, 1, 0))
 
     def send_far(j, carry):
         far_copy(j).start()
         return carry
 
 
-    @pl.when(turning)
-    def _():
-        out_copy.start()
-
-    lax.fori_loop(0, BITS - 1, send_far, 0)
-
-    @pl.when(jnp.logical_not(turning))
-    def _():
-        far_copy(BITS - 1).start()
-
-    load_image.wait()
-    normalize_rows(image_ref, image_mag, own, rows)
+    @pl.when(ahead)
+    def _():
+        load_image.wait()
+        normalize_rows(image_ref, image_mag, own, rows)
+
+    @pl.when(ahead & high)
+    def _():
+        slot_copy(0, own, 0, after).start()
+
+    @pl.when(ahead & low)
+    def _():
+        slot_copy(1, own, 3, before).start()
+
+    lax.fori_loop(0, BITS, send_far, 0)
+
+
+    @pl.when(jnp.logical_not(ahead))
+    def _():
+        load_image.wait()
+        normalize_rows(image_ref, image_mag, own, rows)
+
     targets = [(after, 0), (before, 3), (twin, 1 + core)] + [(near(dy), OWN + 4 - dy) for dy in (1, 2, 3)]
     for i, (device, slot) in enumerate(targets):
         tile_copy(i, OWN, slot, device).start()
-    for i in (3, 4, 5, 2, 0, 1):
+    for i in (3, 4, 5, 2):
         device, slot = targets[i]
         slot_copy(i, own, slot, device).start()
+
+    @pl.when(jnp.logical_not(ahead & high))
+    def _():
+        slot_copy(0, own, 0, after).start()
+
+    @pl.when(jnp.logical_not((ahead & low) | closing_low))
+    def _():
+        slot_copy(1, own, 3, before).start()
+
+    @pl.when(closing_low)
+    def _():
+        edge_copy().start()
 
     held[slot_rows(OWN), :] = own[...]
     image_sum[...] = jnp.zeros_like(image_sum)
@@ -257,7 +302,14 @@
             pass_copy(dy, k).wait_recv()
 
     def relay():
-        slot_copy(6, held.at[slot_rows(source)], source, twin).wait_recv()
+        @pl.when(late & closing_high)
+        def _():
+            closed()
+
+        @pl.when(jnp.logical_not(late & closing_high))
+        def _():
+            slot_copy(6, held.at[slot_rows(source)], source, twin).wait_recv()
+
         slot_copy(6, held.at[slot_rows(source)], place, twin).start()
         tile_copy(6, source, source, twin).wait_recv()
         tile_copy(6, source, place, twin).start()
@@ -265,7 +317,14 @@
     def units(slot, carry):
         @pl.when((slot != OWN) & (slot != source))
         def _():
-            slot_copy(0, own, slot, after).wait_recv()
+            @pl.when(closing_high & (slot == 3 - there))
+            def _():
+                closed()
+
+            @pl.when(jnp.logical_not(closing_high & (slot == 3 - there)))
+            def _():
+                slot_copy(0, own, slot, after).wait_recv()
+
             tile_copy(0, OWN, slot, after).wait_recv()
 
         unit(slot)
@@ -283,15 +342,14 @@
         lax.fori_loop(0, 4, units, 0)
 
     def step(j, carry):
-        @pl.when((j == PIECES - 2) & jnp.logical_not(turning))
-        def _():
-            out_copy.wait_recv()
-            in_copy.start()
-
         far_copy(2 * j).wait_recv()
         far_copy(2 * j + 1).wait_recv()
         for dy in (1, 2, 3):
             pass_copy(dy, j).start()
+
+        @pl.when(closing_low)
+        def _():
+            around_copy(j).start()
 
         text_piece = held[piece(j, 0), :]
         total = jnp.zeros((part, image_ref.shape[1]), jnp.float32)
@@ -315,16 +373,21 @@
 
     lax.fori_loop(0, PIECES, step, 0)
 
-    @pl.when(turning)
-    def _():
-        @pl.when(late)
-        def _():
-            relay()
-
-        lax.fori_loop(0, 4, units, 0)
-
     for k in range(PIECES - LAG, PIECES):
         far_image(k)
+
+    @pl.when(turning)
+    def _():
+        def turned(t, carry):
+            @pl.when((t == 3) & late)
+            def _():
+                relay()
+
+            turn = jnp.where((t < 2) | late, t, 5 - t)
+            return units(jnp.where(low, 3 - turn, turn), carry)
+
+        lax.fori_loop(0, 4, turned, 0)
+
     loss_ref[...] = jnp.sum(loss_sum[...].T, axis=0, keepdims=True)
     backward_rows(image_ref, image_mag, image_sum, None, image_out, 0, rows)
 
@@ -337,7 +400,19 @@
 
     for i, (device, slot) in enumerate(targets):
         tile_copy(i, OWN, slot, device).wait_send()
-        slot_copy(i, own, slot, device).wait_send()
+        if i >= 2:
+            slot_copy(i, own, slot, device).wait_send()
+
+    slot_copy(0, own, 0, after).wait_send()
+
+    @pl.when(jnp.logical_not(closing_low))
+    def _():
+        slot_copy(1, own, 3, before).wait_send()
+
+    @pl.when(closing_low)
+    def _():
+        edge_copy().wait_send()
+
     tile_copy(6, source, place, twin).wait_send()
     slot_copy(6, held.at[slot_rows(source)], place, twin).wait_send()
 
@@ -347,13 +422,14 @@
         far_copy(2 * j).wait_send()
         far_copy(2 * j + 1).wait_send()
         back_copy(j).wait_send()
+
+        @pl.when(closing_low)
+        def _():
+            around_copy(j).wait_send()
+
         return carry
 
     lax.fori_loop(0, PIECES, sent, 0)
-
-    @pl.when(jnp.logical_not(turning))
-    def _():
-        in_copy.wait_send()
 
 
 def on_device(image_emb, text_emb, loop_mask, neg_list):
@@ -385,7 +461,6 @@
             pltpu.VMEM((5, 8, 128), jnp.float32),
             pltpu.VMEM((rows, width), jnp.bfloat16),
             pltpu.VMEM((rows, width), jnp.bfloat16),
-            pltpu.VMEM((rows // BITS, width), jnp.bfloat16),
             pltpu.SemaphoreType.DMA((4,)),
             pltpu.SemaphoreType.DMA((BITS,)),
             pltpu.SemaphoreType.DMA((BITS,)),
@@ -399,6 +474,8 @@
             pltpu.SemaphoreType.DMA((PIECES,)),
             pltpu.SemaphoreType.DMA,
             pltpu.SemaphoreType.DMA,
+            pltpu.SemaphoreType.DMA((PIECES,)),
+            pltpu.SemaphoreType.DMA((PIECES,)),
         ],
         compiler_params=pltpu.CompilerParams(
             collective_id=0, has_side_effects=True, vmem_limit_bytes=60 * 2**20

time: 155 us -> 155 us (level)
  no operation moved by 1% of the time
where the time goes in v4:
time: 155 us
  Pallas kernels  151 us (97%)
  local copies, waits for them, and re-layouts  3.56 us (2%)
    pallas_call x1, Pallas kernels, on_device(): pl.pallas_call(kernel, out_shape=(jax.ShapeDtypeStruct((1, rows), jnp.flo...  151 us
    unnamed x7, local copies, waits for them, and re-layouts  3.56 us

profile of v4, /device:TPU:1, one launch (start us, length us, event | category | flops | bytes accessed | tf_op | source)
XLA Modules:
  0.0 155.3 jit_solution(7310718552116054746)
XLA Ops:
  0.6 151.1 %pair_blocks.1 = (f32[1,128]{1,0:T(1,128)}, bf16[128,1152]{1,0:T(8,128)(2,1)}, bf16[128,1152]{1,0:T(8,128)(2,1)}) custom-call(bf16[128,1152]{1,0:T(8,128)(2,1)} %image_hbm.1, bf16[128,1152]{1,0:T(8,128)(2,1)} %text_hbm.1, s32[1,4]{1,0:T(1,128)} %mask_hbm.1, s32[1,2]{1,0:T(1,128)} %neg_hbm.1), custom_call_target="tpu_custom_call" | custom-call | tf_op jit(solution)/shard_map/pair_blocks/pallas_call | solution.py:439
  151.7 0.0 copy-start.1
  151.7 0.6 copy-done.1
  152.3 0.5 copy.10
  152.8 0.0 copy-start
  152.8 1.7 %copy.11 = bf16[128,1152]{1,0:T(8,128)(2,1)} copy(bf16[128,1152]{1,0:T(8,128)(2,1)} %get-tuple-element.13) | data formatting | bytes 589824
  154.6 0.0 copy-done
  154.6 0.7 copy.12
Async XLA Ops:
  151.7 0.6 copy-start.1
  152.8 1.7 %copy-start = (bf16[128,1152]{1,0:T(8,128)(2,1)S(1)}, bf16[128,1152]{1,0:T(8,128)(2,1)}, u32[]{:S(2)}) copy-start(bf16[128,1152]{1,0:T(8,128)(2,1)} %get-tuple-element.14) | copy-start | bytes 884740
